TPU v7x, 512 devices: a whole 4x4x16 slice. The times are simulated.
512 devices in a mesh: dp: 32 (over y, x, core), cent: 16 (over z).
Axes of the slice: x: 4, y: 4, z: 16, core: 2. Of those that a mesh axis runs over, the one named last changes fastest.
Arguments:
- embeddings: bfloat16 [61440, 1024], P('dp'), may hold values from -32 to 32
- centroids: float32 [2048, 1024], P('cent'), may hold values from -1.5 to 1.5
Outputs:
- new_centroids: float32 [2048, 1024], P('cent')
- row_energy: float32 [61440], P('dp')
All inputs are finite; a program needn't handle non-finite values.
Results may differ from a plain program's by a relative error of at most 0.00075.
Values sent between devices are 32-bit elements; how exact they have to be, the bound alone decides.
A program may use at most 64 MiB of HBM per device.

v0:
```python
import jax
import jax.numpy as jnp
from jax import lax
from jax.sharding import PartitionSpec as P

ITERS = 2


prior_count = 2.0


def iterate(rows, current):
    offset = 0.5 * jnp.sum(current * current, axis=1)
    logits = (
        lax.dot_general(
            rows,
            current,
            (((1,), (1,)), ((), ())),
            precision=lax.Precision.HIGHEST,
            preferred_element_type=jnp.float32,
        )
        - offset[None, :]
    )
    top = lax.pmax(jnp.max(logits, axis=1), "cent")
    total = lax.psum(jnp.sum(jnp.exp(logits - top[:, None]), axis=1), "cent")
    energy = top + jnp.log(total)
    weights = jnp.exp(logits - energy[:, None])
    numer = lax.dot_general(
        weights,
        rows,
        (((0,), (0,)), ((), ())),
        precision=lax.Precision.HIGHEST,
        preferred_element_type=jnp.float32,
    )
    mass = jnp.sum(weights, axis=0)
    numer_all, mass_all = lax.psum((numer, mass), "dp")
    fresh = (numer_all + prior_count * current) / (mass_all + prior_count)[:, None]
    return (fresh, energy)


def local(embeddings, centroids):
    rows = embeddings.astype(jnp.float32)
    current = centroids
    energy = jnp.zeros((embeddings.shape[0],), jnp.float32)
    for step in range(ITERS):
        current, energy = iterate(rows, current)
    return (current, energy)


def solution(mesh):
    in_specs = (P("dp", None), P("cent", None))
    out_specs = (P("cent", None), P("dp"))
    return jax.shard_map(local, mesh=mesh, in_specs=in_specs, out_specs=out_specs, check_vma=False)
```

profile of v0, /device:TPU:1, one launch (start us, length us, event | category | flops | bytes accessed | tf_op | source)
XLA Modules:
  0.0 428.2 jit_solution(810548017749675606)
XLA Ops:
  7.2 0.0 all-reduce.3.cloned.1.call-start
  7.2 1.2 multiply_reduce_fusion.1
  8.4 6.1 %fusion.6 = (f32[1920]{0:T(1024)S(1)}, f32[1920,128]{0,1:T(8,128)S(1)}) fusion(f32[128]{0:T(128)S(1)} %broadcast_multiply_fusion.1, bf16[1920,1024]{1,0:T(8,128)(2,1)} %param.2, f32[128,1024]{1,0:T(8,128)} %param.3), kind=kOutput, calls=%fused_computation.22 | convolution fusion | flops 3020388352 | bytes 5447680 | tf_op jit(solution)/shard_map/dot_general | solution.py:15
  14.5 30.8 %pmax.14 = f32[1920]{0:T(1024)S(1)} all-reduce(f32[1920]{0:T(1024)S(1)} %get-tuple-element.4), channel_id=1, replica_groups=mesh['dp'=32,'cent'=16] {'cent'}, use_global_device_ids=true, to_apply=%region_2.0 | all-reduce | flops 1920 | bytes 15360 | tf_op jit(solution)/shard_map/pmax | solution.py:24
  45.3 0.2 exponential_reduce_fusion.1
  45.4 20.6 %psum.42 = f32[1920]{0:T(1024)S(1)} all-reduce(f32[1920]{0:T(1024)S(1)} %exponential_reduce_fusion.1), channel_id=1, replica_groups=mesh['dp'=32,'cent'=16] {'cent'}, use_global_device_ids=true, to_apply=%region_4.0 | all-reduce | flops 1920 | bytes 15360 | tf_op jit(solution)/shard_map/psum | solution.py:25
  66.0 4.8 %fusion.1 = f32[128,1024]{1,0:T(8,128)} fusion(bf16[1920,1024]{1,0:T(8,128)(2,1)} %param.2, f32[1920,128]{0,1:T(8,128)S(1)} %get-tuple-element.5, f32[1920]{0:T(1024)S(1)} %log_add_fusion.1), kind=kOutput, calls=%fused_computation.7 | convolution fusion | flops 3020144640 | bytes 5447168 | tf_op jit(solution)/shard_map/dot_general | solution.py:28
  70.9 0.0 all-reduce.3.cloned.1.call-update
  70.9 0.0 all-reduce.5.cloned.1.call-start
  70.9 0.2 fusion
  71.2 77.0 %psum.44 = f32[128]{0:T(128)S(1)} all-reduce(f32[128]{0:T(128)S(1)} %fusion), channel_id=1, replica_groups=mesh['dp'=32,'cent'=16] {'dp'}, use_global_device_ids=true, to_apply=%region_7.0 | all-reduce | flops 128 | bytes 1024 | tf_op jit(solution)/shard_map/psum | solution.py:36
  148.1 68.1 %all-reduce.3.cloned.1.call-done = f32[128,1024]{1,0:T(8,128)} async-done(((f32[128,1024]{1,0:T(8,128)}), f32[128,1024]{1,0:T(8,128)}) %all-reduce.3.cloned.1.call-update) | async-done | bytes 524304 | tf_op jit(solution)/shard_map/psum | solution.py:36
  216.2 1.3 multiply_reduce_fusion
  217.5 5.9 %fusion.7 = (f32[1920]{0:T(1024)S(1)}, f32[128,1920]{1,0:T(8,128)S(1)}) fusion(f32[128]{0:T(128)S(1)} %broadcast_multiply_fusion, f32[128,1024]{1,0:T(8,128)S(1)} %get-tuple-element.3, bf16[1920,1024]{1,0:T(8,128)(2,1)} %param.2), kind=kOutput, calls=%fused_computation.23 | convolution fusion | flops 3020388352 | bytes 5447680 | tf_op jit(solution)/shard_map/dot_general | solution.py:15
  223.5 24.9 %pmax.15 = f32[1920]{0:T(1024)S(1)} all-reduce(f32[1920]{0:T(1024)S(1)} %get-tuple-element.6), channel_id=1, replica_groups=mesh['dp'=32,'cent'=16] {'cent'}, use_global_device_ids=true, to_apply=%region_10.0 | all-reduce | flops 1920 | bytes 15360 | tf_op jit(solution)/shard_map/pmax | solution.py:24
  248.4 0.2 exponential_reduce_fusion
  248.6 22.3 %psum.45 = f32[1920]{0:T(1024)S(1)} all-reduce(f32[1920]{0:T(1024)S(1)} %exponential_reduce_fusion), channel_id=1, replica_groups=mesh['dp'=32,'cent'=16] {'cent'}, use_global_device_ids=true, to_apply=%region_12.0 | all-reduce | flops 1920 | bytes 15360 | tf_op jit(solution)/shard_map/psum | solution.py:25
  270.8 0.0 copy-start.1
  270.9 4.8 %fusion.3 = f32[128,1024]{1,0:T(8,128)} fusion(bf16[1920,1024]{1,0:T(8,128)(2,1)} %param.2, f32[128,1920]{1,0:T(8,128)S(1)} %get-tuple-element.7, f32[1920]{0:T(1024)S(1)} %log_add_fusion), kind=kOutput, calls=%fused_computation.9 | convolution fusion | flops 3020144640 | bytes 5447168 | tf_op jit(solution)/shard_map/dot_general | solution.py:28
  275.7 0.0 all-reduce.5.cloned.1.call-update
  275.7 0.2 fusion.2
  275.9 76.4 %psum.47 = f32[128]{0:T(128)S(1)} all-reduce(f32[128]{0:T(128)S(1)} %fusion.2), channel_id=1, replica_groups=mesh['dp'=32,'cent'=16] {'dp'}, use_global_device_ids=true, to_apply=%region_15.0 | all-reduce | flops 128 | bytes 1024 | tf_op jit(solution)/shard_map/psum | solution.py:36
  352.3 67.1 %all-reduce.5.cloned.1.call-done = f32[128,1024]{1,0:T(8,128)} async-done(((f32[128,1024]{1,0:T(8,128)}), f32[128,1024]{1,0:T(8,128)}) %all-reduce.5.cloned.1.call-update) | async-done | bytes 524304 | tf_op jit(solution)/shard_map/psum | solution.py:36
  419.4 1.9 add_divide_fusion
  (9 shorter events, 0.0 us)
Async XLA Ops:
  7.2 209.1 %all-reduce.3.cloned.1.call-start = ((), (), s32[]{:S(2)}) async-start(), calls=%async_computation | async-start | bytes 1048576 | tf_op jit(solution)/shard_map/psum | solution.py:36
  45.3 171.0 %copy-start = (f32[128,1024]{1,0:T(8,128)S(1)}, f32[128,1024]{1,0:T(8,128)}, u32[]{:S(2)}) copy-start(f32[128,1024]{1,0:T(8,128)} %param.3) | copy-start | bytes 1572868
  70.9 348.5 %all-reduce.5.cloned.1.call-start = ((), (), s32[]{:S(2)}) async-start(), calls=%async_computation.1 | async-start | bytes 1048576 | tf_op jit(solution)/shard_map/psum | solution.py:36
  270.8 150.5 %copy-start.1 = (f32[1920]{0:T(1024)}, f32[1920]{0:T(1024)S(1)}, u32[]{:S(2)}) copy-start(f32[1920]{0:T(1024)S(1)} %log_add_fusion) | copy-start | bytes 23044
Sparse Core Ops, SparseCore 0:
  71.0 145.1 all-reduce.2
  275.8 143.5 all-reduce.4
where the time goes:
time: 429 us; the launch traced here: 428 us
  blocking collectives  252 us (59%)
  waiting for transfers between devices  135 us (31%)
  matrix products  21.7 us (5%)
  between operations  14.1 us (3%)
  other arithmetic  5.15 us (1%)
    psum x2, blocking collectives, iterate(): numer_all, mass_all = lax.psum((numer, mass), 'dp')  153 us
    psum x2, waiting for transfers between devices, iterate(): numer_all, mass_all = lax.psum((numer, mass), 'dp')  135 us
    pmax x2, blocking collectives, iterate(): top = lax.pmax(jnp.max(logits, axis=1), 'cent')  55.7 us
    psum x2, blocking collectives, iterate(): total = lax.psum(jnp.sum(jnp.exp(logits - top[:, None]), axis=1), 'cent')  42.8 us
    dot_general x2, matrix products, iterate(): lax.dot_general(rows, current, (((1,), (1,)), ((), ())), precision=lax.Pr...  12 us
    dot_general x2, matrix products, iterate(): lax.dot_general(weights, rows, (((0,), (0,)), ((), ())), precision=lax.Pr...  9.66 us
  transfers between devices with their start and end apart: 2, of which 2 were waited for; matrix products, arithmetic and copies ran while one was open for 0% of the time, Pallas kernels for 0%

commit v1 on v0

v1 whole, which is shorter than its diff:
```python
import jax
import jax.numpy as jnp
from jax import lax
from jax.experimental import pallas as pl
from jax.experimental.pallas import tpu as pltpu
from jax.sharding import PartitionSpec as P

MESH = pl.DeviceIdType.MESH
ITERS = 2
PRIOR = 2.0
N = 4
ZG = 4
ROWS = 1920
D = 1024
K = 128
PIECE = 128
HALF = D // 2
Q = 2
CW = HALF // Q
CHUNKS = ((0, 8), (8, 15))
NT = (((1,), (1,)), ((), ()))
NN = (((1,), (0,)), ((), ()))


def dot(a, b, dims):
    return lax.dot_general(a, b, dims, preferred_element_type=jnp.float32)


def split(v):
    hi = v.astype(jnp.bfloat16)
    lo = (v - hi.astype(jnp.float32)).astype(jnp.bfloat16)
    return hi, lo


def kernel(
    x_hbm, c_hbm, out_c, out_e,
    xv, cur, cs, pbuf, ws, macc, mst, est, zrecv,
    nacc, nsend, crecv, sbuf, arecv, mbuf, mr0, mr1,
    ld, out_sem, z_send, z_recv,
    c_send, c_recv, a_send, a_recv, g_send, g_recv, gc_send, gc_recv,
    m_send, m_recv,
):
    dp = lax.axis_index("dp")
    z = lax.axis_index("cent")
    core = lax.rem(dp, 2)
    chip = dp // 2
    cx = lax.rem(chip, N)
    cy = chip // N
    zg = z // ZG
    zl = lax.rem(z, ZG)
    other = (dp + 1 - 2 * core, z)

    def chip_at(dx, dy):
        return lax.rem(cy + dy, N) * N + lax.rem(cx + dx, N)

    moves = [(dx, dy) for dx in range(N) for dy in range(N) if dx or dy]
    moves.sort(key=lambda v: -(min(v[0], N - v[0]) + min(v[1], N - v[1])))
    chips = [chip_at(dx, dy) for dx, dy in moves]
    planes = [(2 * c + core, z) for c in chips]
    stages = (
        [(dp, zg * ZG + lax.rem(zl + d, ZG)) for d in range(1, ZG)],
        [(dp, lax.rem(zg + d, ZG) * ZG + zl) for d in range(1, ZG)],
    )

    def push(src, dst, send, recv, device):
        pltpu.make_async_remote_copy(
            src_ref=src, dst_ref=dst, send_sem=send, recv_sem=recv,
            device_id=device, device_id_type=MESH,
        ).start()

    def await_bytes(ref, sem):
        pltpu.make_async_copy(ref, ref, sem).wait()

    barrier = pltpu.get_barrier_semaphore()
    peers = [other] + planes + stages[0] + stages[1]
    for device in peers:
        pl.semaphore_signal(barrier, inc=1, device_id=device, device_id_type=MESH)

    load_c = pltpu.make_async_copy(c_hbm, cur.at[0], ld.at[0])
    load_c.start()
    loads = []
    for n, (lo, hi) in enumerate(CHUNKS):
        rows = pl.ds(lo * PIECE, (hi - lo) * PIECE)
        loads.append(pltpu.make_async_copy(x_hbm.at[rows], xv.at[rows], ld.at[n + 1]))
        loads[-1].start()

    def own_cols(q):
        return pl.ds(pl.multiple_of(core * HALF + q * CW, CW), CW)

    def far_cols(q):
        return pl.ds(pl.multiple_of((1 - core) * HALF + q * CW, CW), CW)

    own_half = pl.ds(pl.multiple_of(core * HALF, HALF), HALF)
    far_half = pl.ds(pl.multiple_of((1 - core) * HALF, HALF), HALF)
    base = pl.multiple_of(chip * 8, 8)
    mine = pl.ds(base, 8)

    def split_centroids(it, cols):
        c = cur[it, :, cols]
        hi, lo = split(c)
        cs[0:K, cols] = hi
        cs[K : 2 * K, cols] = lo
        return 0.5 * jnp.sum(c * c, axis=1, keepdims=True)

    def stats(it, n, l, r):
        i = r - CHUNKS[n][0]
        m = jnp.max(l, axis=0, keepdims=True)
        p = jnp.exp(l - m)
        s = jnp.sum(p, axis=0, keepdims=True)
        pbuf[r] = p
        mst[n, i : i + 1] = m
        est[it, n, 0, i : i + 1] = m + jnp.log(s)

    def product(rows, cols):
        both = dot(cs[:, cols], xv[rows, cols], NT)
        return both[0:K] + both[K : 2 * K]

    def logits(it, n):
        lo, hi = CHUNKS[n]
        for r0 in range(lo, hi, 2):
            size = min(2, hi - r0)
            rows = pl.ds(r0 * PIECE, size * PIECE)
            l = product(rows, pl.ds(0, D) if it == 0 else far_half) - offset
            for j in range(size):
                part = l[:, j * PIECE : (j + 1) * PIECE]
                stats(it, n, part if it == 0 else part + pbuf[r0 + j], r0 + j)

    def z_push(it, n, stage):
        for d, device in enumerate(stages[stage]):
            push(est.at[it, n, stage], zrecv.at[it, n, stage, d], z_send.at[it, n, stage], z_recv.at[it, n, stage], device)

    def z_join(it, n, stage):
        await_bytes(zrecv.at[it, n, stage], z_recv.at[it, n, stage])
        e = [est[it, n, stage]] + [zrecv[it, n, stage, d] for d in range(ZG - 1)]
        m = jnp.maximum(jnp.maximum(e[0], e[1]), jnp.maximum(e[2], e[3]))
        s = (jnp.exp(e[0] - m) + jnp.exp(e[1] - m)) + (jnp.exp(e[2] - m) + jnp.exp(e[3] - m))
        est[it, n, stage + 1] = m + jnp.log(s)

    def weigh(it, n):
        lo, hi = CHUNKS[n]
        f = jnp.exp(mst[n] - est[it, n, 2])
        for r in range(lo, hi):
            w = pbuf[r] * f[r - lo : r - lo + 1]
            hi_w, lo_w = split(w)
            cols = pl.ds(r * PIECE, PIECE)
            ws[0:K, cols] = hi_w
            ws[K : 2 * K, cols] = lo_w
            macc[...] += w

    def numer(n, cols):
        lo, hi = CHUNKS[n]
        rows = pl.ds(lo * PIECE, (hi - lo) * PIECE)
        both = dot(ws[:, rows], xv[rows, cols], NN)
        return both[0:K] + both[K : 2 * K]

    for n, (lo, hi) in enumerate(CHUNKS):
        if hi - lo < 8:
            mst[n, hi - lo : 8] = jnp.zeros((8 - hi + lo, PIECE), jnp.float32)
            for it in range(ITERS):
                est[it, n, 0, hi - lo : 8] = jnp.zeros((8 - hi + lo, PIECE), jnp.float32)

    load_c.wait()
    offset = split_centroids(0, pl.ds(0, D))
    for it in range(ITERS):
        for n in range(2):
            if it == 0:
                loads[n].wait()
            logits(it, n)
            if it == 0 and n == 0:
                pl.semaphore_wait(barrier, len(peers))
            z_push(it, n, 0)
        macc[...] = jnp.zeros_like(macc)
        for n in range(2):
            z_join(it, n, 0)
            z_push(it, n, 1)
        z_join(it, 0, 1)
        weigh(it, 0)
        for q in range(Q):
            nacc[:, far_cols(q)] = numer(0, far_cols(q))
        for q in range(Q):
            nacc[:, own_cols(q)] = numer(0, own_cols(q))
        z_join(it, 1, 1)
        weigh(it, 1)

        mass = jnp.sum(macc[...], axis=1, keepdims=True)
        eye = lax.broadcasted_iota(jnp.int32, (K, K), 0) == lax.broadcasted_iota(jnp.int32, (K, K), 1)
        mbuf[it, 0] = jnp.sum(jnp.where(eye, mass, 0.0), axis=0, keepdims=True)
        push(mbuf.at[it, 0], mr0.at[it, 0], m_send.at[it, 0], m_recv.at[it, 0], other)

        for q in range(Q):
            nsend[it, q] = nacc[:, far_cols(q)] + numer(1, far_cols(q))
            push(nsend.at[it, q], crecv.at[it, q], c_send.at[it, q], c_recv.at[it, q], other)

        for q in range(Q):
            part = nacc[:, own_cols(q)] + numer(1, own_cols(q))
            await_bytes(crecv.at[it, q], c_recv.at[it, q])
            sbuf[it, q] = part + crecv[it, q]
            for d, (c, device) in enumerate(zip(chips, planes)):
                rows = pl.ds(pl.multiple_of(c * 8, 8), 8)
                push(sbuf.at[it, q, rows], arecv.at[it, q, d], a_send.at[it, q], a_recv.at[it, q], device)
            if q == 0:
                await_bytes(mr0.at[it, 0], m_recv.at[it, 0])
                mbuf[it, 1] = mbuf[it, 0] + mr0[it, 0]
                for d, device in enumerate(planes):
                    push(mbuf.at[it, 1], mr1.at[it, d], m_send.at[it, 1], m_recv.at[it, 1], device)

        await_bytes(mr1.at[it], m_recv.at[it, 1])
        total = mbuf[it, 1] + jnp.sum(mr1[it], axis=0)
        lane = lax.broadcasted_iota(jnp.int32, (8, K), 1)
        want = lax.broadcasted_iota(jnp.int32, (8, K), 0) + base
        denom = jnp.sum(jnp.where(lane == want, total, 0.0), axis=1, keepdims=True) + PRIOR

        for q in range(Q):
            await_bytes(arecv.at[it, q], a_recv.at[it, q])
            got = sbuf[it, q, mine] + jnp.sum(arecv[it, q], axis=0)
            cols = own_cols(q)
            cur[it + 1, mine, cols] = (got + PRIOR * cur[it, mine, cols]) / denom
            block = cur.at[it + 1, mine, cols]
            for device in planes:
                push(block, block, g_send.at[it, q], g_recv.at[it, q], device)
        for q in range(Q):
            await_bytes(cur.at[it + 1, pl.ds(0, 120), own_cols(q)], g_recv.at[it, q])
            block = cur.at[it + 1, :, own_cols(q)]
            push(block, block, gc_send.at[it, q], gc_recv.at[it, q], other)

        if it + 1 < ITERS:
            offset = split_centroids(it + 1, own_half)
            for r0 in range(0, ROWS // PIECE, 2):
                size = min(2, ROWS // PIECE - r0)
                l = product(pl.ds(r0 * PIECE, size * PIECE), own_half)
                for j in range(size):
                    pbuf[r0 + j] = l[:, j * PIECE : (j + 1) * PIECE]
            for q in range(Q):
                await_bytes(cur.at[it + 1, :, far_cols(q)], gc_recv.at[it, q])
            offset = offset + split_centroids(it + 1, far_half)

    last = ITERS
    outs = []

    def store(cols, i):
        copy = pltpu.make_async_copy(cur.at[last, :, cols], out_c.at[:, cols], out_sem.at[i])
        copy.start()
        outs.append(copy)

    for q in range(Q):
        store(own_cols(q), q)
    for n, (lo, hi) in enumerate(CHUNKS):
        out_e[lo:hi] = est[ITERS - 1, n, 2, 0 : hi - lo]
    for q in range(Q):
        await_bytes(cur.at[last, :, far_cols(q)], gc_recv.at[ITERS - 1, q])
        store(far_cols(q), Q + q)

    for it in range(ITERS):
        for n in range(2):
            for stage in range(2):
                await_bytes(zrecv.at[it, n, stage], z_send.at[it, n, stage])
        await_bytes(mr0.at[it, 0], m_send.at[it, 0])
        await_bytes(mr1.at[it], m_send.at[it, 1])
        for q in range(Q):
            await_bytes(crecv.at[it, q], c_send.at[it, q])
            await_bytes(arecv.at[it, q], a_send.at[it, q])
            await_bytes(arecv.at[it, q], g_send.at[it, q])
            await_bytes(crecv.at[it, q], gc_send.at[it, q])
    for copy in outs:
        copy.wait()


def local(embeddings, centroids):
    f32, bf16 = jnp.float32, jnp.bfloat16
    pieces = ROWS // PIECE
    vm = pltpu.VMEM
    dma = pltpu.SemaphoreType.DMA
    new, energy = pl.pallas_call(
        kernel,
        out_shape=(
            jax.ShapeDtypeStruct((K, D), f32),
            jax.ShapeDtypeStruct((pieces, PIECE), f32),
        ),
        in_specs=[pl.BlockSpec(memory_space=pl.ANY)] * 2,
        out_specs=(pl.BlockSpec(memory_space=pl.ANY), pl.BlockSpec(memory_space=pltpu.VMEM)),
        scratch_shapes=[
            vm((ROWS, D), bf16),
            vm((ITERS + 1, K, D), f32),
            vm((2 * K, D), bf16),
            vm((pieces, K, PIECE), f32),
            vm((2 * K, ROWS), bf16),
            vm((K, PIECE), f32),
            vm((2, 8, PIECE), f32),
            vm((ITERS, 2, 3, 8, PIECE), f32),
            vm((ITERS, 2, 2, ZG - 1, 8, PIECE), f32),
            vm((K, D), f32),
            vm((ITERS, Q, K, CW), f32),
            vm((ITERS, Q, K, CW), f32),
            vm((ITERS, Q, K, CW), f32),
            vm((ITERS, Q, N * N - 1, 8, CW), f32),
            vm((ITERS, 2, 1, K), f32),
            vm((ITERS, 1, 1, K), f32),
            vm((ITERS, N * N - 1, 1, K), f32),
            dma((3,)),
            dma((2 * Q,)),
            dma((ITERS, 2, 2)),
            dma((ITERS, 2, 2)),
        ]
        + [dma((ITERS, Q))] * 8
        + [dma((ITERS, 2))] * 2,
        compiler_params=pltpu.CompilerParams(
            collective_id=0, has_side_effects=True, vmem_limit_bytes=53 * 1024 * 1024
        ),
        cost_estimate=pl.CostEstimate(flops=4 * 10**9, bytes_accessed=5 * 10**6, transcendentals=10**6),
    )(embeddings, centroids)
    return new, energy.reshape(ROWS)


def solution(mesh):
    in_specs = (P("dp", None), P("cent", None))
    out_specs = (P("cent", None), P("dp"))
    return jax.shard_map(local, mesh=mesh, in_specs=in_specs, out_specs=out_specs, check_vma=False)
```

time: 429 us -> 72.7 us (0.17)
  blocking collectives: 252 us -> 0 us
  waiting for transfers between devices: 135 us -> 0 us
  Pallas kernels: 0 us -> 70.6 us
  matrix products: 21.7 us -> 0 us
  between operations: 14.1 us -> 0.64 us
  other arithmetic: 5.15 us -> 0 us
    psum x4 -> x0, blocking collectives: 196 us -> none  [the longest x2 153 us: iterate(): numer_all, mass_all = lax.psum((numer, mass), 'dp')]
    psum x2 -> x0, waiting for transfers between devices: 135 us -> none  [iterate(): numer_all, mass_all = lax.psum((numer, mass), 'dp')]
    pallas_call x0 -> x1, Pallas kernels: none -> 70.6 us  [local(): pl.pallas_call(kernel, out_shape=(jax.ShapeDtypeStruct((K, D), f32), jax....]
    pmax x2 -> x0, blocking collectives: 55.7 us -> none  [iterate(): top = lax.pmax(jnp.max(logits, axis=1), 'cent')]
    dot_general x4 -> x0, matrix products: 21.7 us -> none  [the longest x2 12 us: iterate(): lax.dot_general(rows, current, (((1,), (1,)), ((), ())), precision=lax.Pr...]
  transfers between devices with their start and end apart: 2 -> 0, of which waited for: 2 -> 0; matrix products, arithmetic and copies ran while one was open for 0% -> 0% of each run, Pallas kernels for 0% -> 0%
where the time goes in v1:
time: 72.7 us; the launch traced here: 72.6 us
  Pallas kernels  70.6 us (97%)
  local copies, waits for them, and re-layouts  1.39 us (2%)
    pallas_call x1, Pallas kernels, local(): pl.pallas_call(kernel, out_shape=(jax.ShapeDtypeStruct((K, D), f32), jax....  70.6 us

profile of v1, /device:TPU:1, one launch (start us, length us, event | category | flops | bytes accessed | tf_op | source)
XLA Modules:
  0.0 72.6 jit_solution(10255724739638382495)
XLA Ops:
  0.6 70.6 %shard_map.41 = (f32[128,1024]{1,0:T(8,128)S(1)}, f32[15,128]{1,0:T(8,128)S(1)}) custom-call(bf16[1920,1024]{1,0:T(8,128)(2,1)} %x_hbm.1, f32[128,1024]{1,0:T(8,128)} %c_hbm.1), custom_call_target="tpu_custom_call" | custom-call | flops 4000000000 | bytes 5000000 | tf_op jit(solution)/shard_map/pallas_call | solution.py:273
  71.2 0.8 %copy.6 = f32[128,1024]{1,0:T(8,128)} copy(f32[128,1024]{1,0:T(8,128)S(1)} %get-tuple-element.8) | data formatting | bytes 1048576
  72.0 0.6 copy.7

commit v2 on v1

v2 whole, which is shorter than its diff:
```python
import jax
import jax.numpy as jnp
from jax import lax
from jax.experimental import pallas as pl
from jax.experimental.pallas import tpu as pltpu
from jax.sharding import PartitionSpec as P

MESH = pl.DeviceIdType.MESH
ITERS = 2
PRIOR = 2.0
N = 4
PLANE = N * N - 1
Z = 16
ROWS = 1920
D = 1024
K = 128
PIECE = 128
HALF = D // 2
Q = 2
CW = HALF // Q
CHUNKS = ((0, 8), (8, 15))
NT = (((1,), (1,)), ((), ()))
NN = (((1,), (0,)), ((), ()))


def dot(a, b, dims):
    return lax.dot_general(a, b, dims, preferred_element_type=jnp.float32)


def split(v):
    hi = v.astype(jnp.bfloat16)
    lo = (v - hi.astype(jnp.float32)).astype(jnp.bfloat16)
    return hi, lo


def kernel(
    x_hbm, c_hbm, out_c, out_e,
    xv, cur, cs, pbuf, ws, macc, mst, est, energy, zrecv,
    nacc, nbuf, crecv, sbuf, drecv, arecv, mbuf, mrecv,
    ld, z_send, z_recv,
    c_send, c_recv, a_send, a_recv, g_send, g_recv, gc_send, gc_recv, far_recv,
    m_send, m_recv,
):
    dp = lax.axis_index("dp")
    z = lax.axis_index("cent")
    core = lax.rem(dp, 2)
    chip = dp // 2
    cx = lax.rem(chip, N)
    cy = chip // N
    other = (dp + 1 - 2 * core, z)

    def chip_at(dx, dy):
        return lax.rem(cy + dy, N) * N + lax.rem(cx + dx, N)

    moves = [(dx, dy) for dx in range(N) for dy in range(N) if dx or dy]
    moves.sort(key=lambda v: -(min(v[0], N - v[0]) + min(v[1], N - v[1])))
    chips = [chip_at(dx, dy) for dx, dy in moves]
    planes = [(2 * c + core, z) for c in chips]
    cross = [(2 * c + 1 - core, z) for c in chips] + [other]
    places = [pl.ds(pl.multiple_of(c * 8, 8), 8) for c in chips + [chip]]
    along_z = [(dp, lax.rem(z + d, Z)) for d in sorted(range(1, Z), key=lambda d: -min(d, Z - d))]

    def push(src, dst, send, recv, device):
        pltpu.make_async_remote_copy(
            src_ref=src, dst_ref=dst, send_sem=send, recv_sem=recv,
            device_id=device, device_id_type=MESH,
        ).start()

    def await_bytes(ref, sem):
        pltpu.make_async_copy(ref, ref, sem).wait()

    barrier = pltpu.get_barrier_semaphore()
    peers = planes + cross + along_z
    for device in peers:
        pl.semaphore_signal(barrier, inc=1, device_id=device, device_id_type=MESH)

    load_c = pltpu.make_async_copy(c_hbm, cur.at[0], ld.at[0])
    load_c.start()
    loads = []
    for n, (lo, hi) in enumerate(CHUNKS):
        rows = pl.ds(lo * PIECE, (hi - lo) * PIECE)
        loads.append(pltpu.make_async_copy(x_hbm.at[rows], xv.at[rows], ld.at[n + 1]))
        loads[-1].start()

    def own_cols(q):
        return pl.ds(pl.multiple_of(core * HALF + q * CW, CW), CW)

    def far_cols(q):
        return pl.ds(pl.multiple_of((1 - core) * HALF + q * CW, CW), CW)

    far_half = pl.ds(pl.multiple_of((1 - core) * HALF, HALF), HALF)
    base = pl.multiple_of(chip * 8, 8)
    mine = pl.ds(base, 8)

    def split_centroids(it, cols):
        c = cur[it, :, cols]
        hi, lo = split(c)
        cs[0:K, cols] = hi
        cs[K : 2 * K, cols] = lo
        return 0.5 * jnp.sum(c * c, axis=1, keepdims=True)

    def stats(it, n, l, r):
        i = r - CHUNKS[n][0]
        m = jnp.max(l, axis=0, keepdims=True)
        p = jnp.exp(l - m)
        s = jnp.sum(p, axis=0, keepdims=True)
        pbuf[r] = p
        mst[n, i : i + 1] = m
        est[it, n, i : i + 1] = m + jnp.log(s)

    def product(rows, cols):
        both = dot(cs[:, cols], xv[rows, cols], NT)
        return both[0:K] + both[K : 2 * K]

    def logits(it, n):
        lo, hi = CHUNKS[n]
        for r0 in range(lo, hi, 2):
            size = min(2, hi - r0)
            rows = pl.ds(r0 * PIECE, size * PIECE)
            if it == 0:
                l = product(rows, pl.ds(0, D)) - offset
            else:
                l = product(rows, far_half) + product(rows, own_cols(1)) - offset
            for j in range(size):
                part = l[:, j * PIECE : (j + 1) * PIECE]
                stats(it, n, part if it == 0 else part + pbuf[r0 + j], r0 + j)

    def z_push(it, n):
        for device in along_z:
            push(est.at[it, n], zrecv.at[it, n, z], z_send.at[it, n], z_recv.at[it, n], device)
        zrecv[it, n, z] = est[it, n]

    def z_join(it, n):
        await_bytes(zrecv.at[it, n, pl.ds(0, Z - 1)], z_recv.at[it, n])
        e = zrecv[it, n]
        m = jnp.max(e, axis=0)
        energy[it, n] = m + jnp.log(jnp.sum(jnp.exp(e - m[None]), axis=0))

    def weigh(it, n):
        lo, hi = CHUNKS[n]
        f = jnp.exp(mst[n] - energy[it, n])
        for r in range(lo, hi):
            w = pbuf[r] * f[r - lo : r - lo + 1]
            hi_w, lo_w = split(w)
            cols = pl.ds(r * PIECE, PIECE)
            ws[0:K, cols] = hi_w
            ws[K : 2 * K, cols] = lo_w
            macc[...] += w

    def numer(n, cols):
        lo, hi = CHUNKS[n]
        rows = pl.ds(lo * PIECE, (hi - lo) * PIECE)
        both = dot(ws[:, rows], xv[rows, cols], NN)
        return both[0:K] + both[K : 2 * K]

    for n, (lo, hi) in enumerate(CHUNKS):
        if hi - lo < 8:
            mst[n, hi - lo : 8] = jnp.zeros((8 - hi + lo, PIECE), jnp.float32)
            for it in range(ITERS):
                est[it, n, hi - lo : 8] = jnp.zeros((8 - hi + lo, PIECE), jnp.float32)

    load_c.wait()
    offset = split_centroids(0, pl.ds(0, D))
    for it in range(ITERS):
        for n in range(2):
            if it == 0:
                loads[n].wait()
            logits(it, n)
            if it == 0 and n == 0:
                pl.semaphore_wait(barrier, len(peers))
            z_push(it, n)
        macc[...] = jnp.zeros_like(macc)
        z_join(it, 0)
        weigh(it, 0)
        for q in range(Q):
            nacc[:, far_cols(q)] = numer(0, far_cols(q))
        for q in range(Q):
            nacc[:, own_cols(q)] = numer(0, own_cols(q))
        z_join(it, 1)
        weigh(it, 1)

        mass = jnp.sum(macc[...], axis=1, keepdims=True)
        eye = lax.broadcasted_iota(jnp.int32, (K, K), 0) == lax.broadcasted_iota(jnp.int32, (K, K), 1)
        mbuf[it] = jnp.sum(jnp.where(eye, mass, 0.0), axis=0, keepdims=True)

        def total_numer(cols):
            return nacc[:, cols] + numer(1, cols)

        nbuf[it, 2] = total_numer(far_cols(1))
        push(nbuf.at[it, 2], crecv.at[it], c_send.at[it], c_recv.at[it], other)
        nbuf[it, 0] = total_numer(own_cols(0))
        for d, device in enumerate(planes):
            push(nbuf.at[it, 0, places[d]], drecv.at[it, d], a_send.at[it, 0], a_recv.at[it, 0], device)
        nbuf[it, 1] = total_numer(far_cols(0))
        for d, device in enumerate(cross):
            push(nbuf.at[it, 1, places[d]], drecv.at[it, PLANE + d], a_send.at[it, 0], a_recv.at[it, 0], device)
        for d, device in enumerate(planes + cross):
            push(mbuf.at[it], mrecv.at[it, d], m_send.at[it], m_recv.at[it], device)
        part = total_numer(own_cols(1))
        await_bytes(crecv.at[it], c_recv.at[it])
        sbuf[it] = part + crecv[it]
        for d, device in enumerate(planes):
            push(sbuf.at[it, places[d]], arecv.at[it, d], a_send.at[it, 1], a_recv.at[it, 1], device)

        await_bytes(mrecv.at[it], m_recv.at[it])
        total = mbuf[it] + jnp.sum(mrecv[it], axis=0)
        lane = lax.broadcasted_iota(jnp.int32, (8, K), 1)
        want = lax.broadcasted_iota(jnp.int32, (8, K), 0) + base
        denom = jnp.sum(jnp.where(lane == want, total, 0.0), axis=1, keepdims=True) + PRIOR

        fresh = cur.at[it + 1] if it + 1 < ITERS else out_c

        def update(q, got):
            cols = own_cols(q)
            fresh[mine, cols] = (got + PRIOR * cur[it, mine, cols]) / denom
            block = fresh.at[mine, cols]
            for device in planes:
                push(block, block, g_send.at[it, q], g_recv.at[it, q], device)
            return block

        await_bytes(drecv.at[it], a_recv.at[it, 0])
        update(0, nbuf[it, 0, mine] + jnp.sum(drecv[it], axis=0))
        await_bytes(arecv.at[it], a_recv.at[it, 1])
        block = update(1, sbuf[it, mine] + jnp.sum(arecv[it], axis=0))
        for device in cross:
            push(block, block, g_send.at[it, 2], far_recv.at[it], device)

        await_bytes(fresh.at[pl.ds(0, 8 * PLANE), own_cols(0)], g_recv.at[it, 0])
        block = fresh.at[:, own_cols(0)]
        push(block, block, gc_send.at[it], gc_recv.at[it], other)
        if it + 1 < ITERS:
            offset = split_centroids(it + 1, own_cols(0))
            for r0 in range(0, ROWS // PIECE, 2):
                size = min(2, ROWS // PIECE - r0)
                l = product(pl.ds(r0 * PIECE, size * PIECE), own_cols(0))
                for j in range(size):
                    pbuf[r0 + j] = l[:, j * PIECE : (j + 1) * PIECE]
        await_bytes(fresh.at[pl.ds(0, 8 * PLANE), own_cols(1)], g_recv.at[it, 1])
        await_bytes(fresh.at[:, far_cols(1)], far_recv.at[it])
        await_bytes(fresh.at[:, far_cols(0)], gc_recv.at[it])
        if it + 1 < ITERS:
            offset = offset + split_centroids(it + 1, own_cols(1)) + split_centroids(it + 1, far_half)

    for n, (lo, hi) in enumerate(CHUNKS):
        out_e[lo:hi] = energy[ITERS - 1, n, 0 : hi - lo]

    for it in range(ITERS):
        for n in range(2):
            await_bytes(zrecv.at[it, n, pl.ds(0, Z - 1)], z_send.at[it, n])
        await_bytes(mrecv.at[it], m_send.at[it])
        await_bytes(crecv.at[it], c_send.at[it])
        await_bytes(drecv.at[it], a_send.at[it, 0])
        for q in range(Q):
            await_bytes(arecv.at[it], g_send.at[it, q])
        await_bytes(arecv.at[it], a_send.at[it, 1])
        await_bytes(sbuf.at[it, pl.ds(0, 8 * PLANE + 8)], g_send.at[it, 2])
        await_bytes(crecv.at[it], gc_send.at[it])


def local(embeddings, centroids):
    f32, bf16 = jnp.float32, jnp.bfloat16
    pieces = ROWS // PIECE
    vm = pltpu.VMEM
    dma = pltpu.SemaphoreType.DMA
    new, energy = pl.pallas_call(
        kernel,
        out_shape=(
            jax.ShapeDtypeStruct((K, D), f32),
            jax.ShapeDtypeStruct((pieces, PIECE), f32),
        ),
        in_specs=[pl.BlockSpec(memory_space=pl.ANY)] * 2,
        out_specs=(pl.BlockSpec(memory_space=pltpu.VMEM),) * 2,
        scratch_shapes=[
            vm((ROWS, D), bf16),
            vm((ITERS, K, D), f32),
            vm((2 * K, D), bf16),
            vm((pieces, K, PIECE), f32),
            vm((2 * K, ROWS), bf16),
            vm((K, PIECE), f32),
            vm((2, 8, PIECE), f32),
            vm((ITERS, 2, 8, PIECE), f32),
            vm((ITERS, 2, 8, PIECE), f32),
            vm((ITERS, 2, Z, 8, PIECE), f32),
            vm((K, D), f32),
            vm((ITERS, 3, K, CW), f32),
            vm((ITERS, K, CW), f32),
            vm((ITERS, K, CW), f32),
            vm((ITERS, 2 * PLANE + 1, 8, CW), f32),
            vm((ITERS, PLANE, 8, CW), f32),
            vm((ITERS, 1, K), f32),
            vm((ITERS, 2 * PLANE + 1, 1, K), f32),
            dma((3,)),
            dma((ITERS, 2)),
            dma((ITERS, 2)),
        ]
        + [dma((ITERS,))] * 2
        + [dma((ITERS, 2))] * 2
        + [dma((ITERS, 3))] * 2
        + [dma((ITERS,))] * 5,
        compiler_params=pltpu.CompilerParams(
            collective_id=0, has_side_effects=True, vmem_limit_bytes=53 * 1024 * 1024
        ),
        cost_estimate=pl.CostEstimate(flops=4 * 10**9, bytes_accessed=5 * 10**6, transcendentals=10**6),
    )(embeddings, centroids)
    return new, energy.reshape(ROWS)


def solution(mesh):
    in_specs = (P("dp", None), P("cent", None))
    out_specs = (P("cent", None), P("dp"))
    return jax.shard_map(local, mesh=mesh, in_specs=in_specs, out_specs=out_specs, check_vma=False)
```

time: 72.7 us -> 71.5 us (0.983)
  Pallas kernels: 70.6 us -> 69.4 us
    pallas_call x1, Pallas kernels: 70.6 us -> 69.4 us  [local(): pl.pallas_call(kernel, out_shape=(jax.ShapeDtypeStruct((K, D), f32), jax....]
where the time goes in v2:
time: 71.5 us; the launch traced here: 71.4 us
  Pallas kernels  69.4 us (97%)
  local copies, waits for them, and re-layouts  1.39 us (2%)
    pallas_call x1, Pallas kernels, local(): pl.pallas_call(kernel, out_shape=(jax.ShapeDtypeStruct((K, D), f32), jax....  69.4 us

profile of v2, /device:TPU:1, one launch (start us, length us, event | category | flops | bytes accessed | tf_op | source)
XLA Modules:
  0.0 71.4 jit_solution(12494817394821222619)
XLA Ops:
  0.6 69.4 %shard_map.41 = (f32[128,1024]{1,0:T(8,128)S(1)}, f32[15,128]{1,0:T(8,128)S(1)}) custom-call(bf16[1920,1024]{1,0:T(8,128)(2,1)} %x_hbm.1, f32[128,1024]{1,0:T(8,128)} %c_hbm.1), custom_call_target="tpu_custom_call" | custom-call | flops 4000000000 | bytes 5000000 | tf_op jit(solution)/shard_map/pallas_call | solution.py:265
  70.0 0.8 %copy.6 = f32[128,1024]{1,0:T(8,128)} copy(f32[128,1024]{1,0:T(8,128)S(1)} %get-tuple-element.8) | data formatting | bytes 1048576
  70.8 0.6 copy.7

commit v3 on v1

--- a/solution.py
+++ b/solution.py
@@ -9,7 +9,7 @@
 ITERS = 2
 PRIOR = 2.0
 N = 4
-ZG = 4
+Z = 16
 ROWS = 1920
 D = 1024
 K = 128
@@ -34,9 +34,9 @@
 
 def kernel(
     x_hbm, c_hbm, out_c, out_e,
-    xv, cur, cs, pbuf, ws, macc, mst, est, zrecv,
+    xv, cur, cs, pbuf, ws, macc, mst, est, energy, zrecv,
     nacc, nsend, crecv, sbuf, arecv, mbuf, mr0, mr1,
-    ld, out_sem, z_send, z_recv,
+    ld, z_send, z_recv,
     c_send, c_recv, a_send, a_recv, g_send, g_recv, gc_send, gc_recv,
     m_send, m_recv,
 ):
@@ -46,8 +46,6 @@
     chip = dp // 2
     cx = lax.rem(chip, N)
     cy = chip // N
-    zg = z // ZG
-    zl = lax.rem(z, ZG)
     other = (dp + 1 - 2 * core, z)
 
     def chip_at(dx, dy):
@@ -57,10 +55,7 @@
     moves.sort(key=lambda v: -(min(v[0], N - v[0]) + min(v[1], N - v[1])))
     chips = [chip_at(dx, dy) for dx, dy in moves]
     planes = [(2 * c + core, z) for c in chips]
-    stages = (
-        [(dp, zg * ZG + lax.rem(zl + d, ZG)) for d in range(1, ZG)],
-        [(dp, lax.rem(zg + d, ZG) * ZG + zl) for d in range(1, ZG)],
-    )
+    along_z = [(dp, lax.rem(z + d, Z)) for d in sorted(range(1, Z), key=lambda d: -min(d, Z - d))]
 
     def push(src, dst, send, recv, device):
         pltpu.make_async_remote_copy(
@@ -71,18 +66,18 @@
     def await_bytes(ref, sem):
         pltpu.make_async_copy(ref, ref, sem).wait()
 
-    barrier = pltpu.get_barrier_semaphore()
-    peers = [other] + planes + stages[0] + stages[1]
-    for device in peers:
-        pl.semaphore_signal(barrier, inc=1, device_id=device, device_id_type=MESH)
-
     load_c = pltpu.make_async_copy(c_hbm, cur.at[0], ld.at[0])
     load_c.start()
     loads = []
-    for n, (lo, hi) in enumerate(CHUNKS):
-        rows = pl.ds(lo * PIECE, (hi - lo) * PIECE)
-        loads.append(pltpu.make_async_copy(x_hbm.at[rows], xv.at[rows], ld.at[n + 1]))
+    for r0 in range(0, ROWS // PIECE, 2):
+        rows = pl.ds(r0 * PIECE, min(2, ROWS // PIECE - r0) * PIECE)
+        loads.append(pltpu.make_async_copy(x_hbm.at[rows], xv.at[rows], ld.at[1 + r0 // 2]))
         loads[-1].start()
+
+    barrier = pltpu.get_barrier_semaphore()
+    peers = [other] + planes + along_z
+    for device in peers:
+        pl.semaphore_signal(barrier, inc=1, device_id=device, device_id_type=MESH)
 
     def own_cols(q):
         return pl.ds(pl.multiple_of(core * HALF + q * CW, CW), CW)
@@ -109,7 +104,7 @@
         s = jnp.sum(p, axis=0, keepdims=True)
         pbuf[r] = p
         mst[n, i : i + 1] = m
-        est[it, n, 0, i : i + 1] = m + jnp.log(s)
+        est[it, n, i : i + 1] = m + jnp.log(s)
 
     def product(rows, cols):
         both = dot(cs[:, cols], xv[rows, cols], NT)
@@ -120,25 +115,27 @@
         for r0 in range(lo, hi, 2):
             size = min(2, hi - r0)
             rows = pl.ds(r0 * PIECE, size * PIECE)
+            if it == 0:
+                loads[r0 // 2].wait()
             l = product(rows, pl.ds(0, D) if it == 0 else far_half) - offset
             for j in range(size):
                 part = l[:, j * PIECE : (j + 1) * PIECE]
                 stats(it, n, part if it == 0 else part + pbuf[r0 + j], r0 + j)
 
-    def z_push(it, n, stage):
-        for d, device in enumerate(stages[stage]):
-            push(est.at[it, n, stage], zrecv.at[it, n, stage, d], z_send.at[it, n, stage], z_recv.at[it, n, stage], device)
-
-    def z_join(it, n, stage):
-        await_bytes(zrecv.at[it, n, stage], z_recv.at[it, n, stage])
-        e = [est[it, n, stage]] + [zrecv[it, n, stage, d] for d in range(ZG - 1)]
-        m = jnp.maximum(jnp.maximum(e[0], e[1]), jnp.maximum(e[2], e[3]))
-        s = (jnp.exp(e[0] - m) + jnp.exp(e[1] - m)) + (jnp.exp(e[2] - m) + jnp.exp(e[3] - m))
-        est[it, n, stage + 1] = m + jnp.log(s)
+    def z_push(it, n):
+        for device in along_z:
+            push(est.at[it, n], zrecv.at[it, n, z], z_send.at[it, n], z_recv.at[it, n], device)
+        zrecv[it, n, z] = est[it, n]
+
+    def z_join(it, n):
+        await_bytes(zrecv.at[it, n, pl.ds(0, Z - 1)], z_recv.at[it, n])
+        e = zrecv[it, n]
+        m = jnp.max(e, axis=0)
+        energy[it, n] = m + jnp.log(jnp.sum(jnp.exp(e - m[None]), axis=0))
 
     def weigh(it, n):
         lo, hi = CHUNKS[n]
-        f = jnp.exp(mst[n] - est[it, n, 2])
+        f = jnp.exp(mst[n] - energy[it, n])
         for r in range(lo, hi):
             w = pbuf[r] * f[r - lo : r - lo + 1]
             hi_w, lo_w = split(w)
@@ -157,29 +154,24 @@
         if hi - lo < 8:
             mst[n, hi - lo : 8] = jnp.zeros((8 - hi + lo, PIECE), jnp.float32)
             for it in range(ITERS):
-                est[it, n, 0, hi - lo : 8] = jnp.zeros((8 - hi + lo, PIECE), jnp.float32)
+                est[it, n, hi - lo : 8] = jnp.zeros((8 - hi + lo, PIECE), jnp.float32)
 
     load_c.wait()
     offset = split_centroids(0, pl.ds(0, D))
     for it in range(ITERS):
         for n in range(2):
-            if it == 0:
-                loads[n].wait()
             logits(it, n)
             if it == 0 and n == 0:
                 pl.semaphore_wait(barrier, len(peers))
-            z_push(it, n, 0)
+            z_push(it, n)
         macc[...] = jnp.zeros_like(macc)
-        for n in range(2):
-            z_join(it, n, 0)
-            z_push(it, n, 1)
-        z_join(it, 0, 1)
+        z_join(it, 0)
         weigh(it, 0)
         for q in range(Q):
             nacc[:, far_cols(q)] = numer(0, far_cols(q))
         for q in range(Q):
             nacc[:, own_cols(q)] = numer(0, own_cols(q))
-        z_join(it, 1, 1)
+        z_join(it, 1)
         weigh(it, 1)
 
         mass = jnp.sum(macc[...], axis=1, keepdims=True)
@@ -210,17 +202,18 @@
         want = lax.broadcasted_iota(jnp.int32, (8, K), 0) + base
         denom = jnp.sum(jnp.where(lane == want, total, 0.0), axis=1, keepdims=True) + PRIOR
 
+        fresh = cur.at[it + 1] if it + 1 < ITERS else out_c
         for q in range(Q):
             await_bytes(arecv.at[it, q], a_recv.at[it, q])
             got = sbuf[it, q, mine] + jnp.sum(arecv[it, q], axis=0)
             cols = own_cols(q)
-            cur[it + 1, mine, cols] = (got + PRIOR * cur[it, mine, cols]) / denom
-            block = cur.at[it + 1, mine, cols]
+            fresh[mine, cols] = (got + PRIOR * cur[it, mine, cols]) / denom
+            block = fresh.at[mine, cols]
             for device in planes:
                 push(block, block, g_send.at[it, q], g_recv.at[it, q], device)
         for q in range(Q):
-            await_bytes(cur.at[it + 1, pl.ds(0, 120), own_cols(q)], g_recv.at[it, q])
-            block = cur.at[it + 1, :, own_cols(q)]
+            await_bytes(fresh.at[pl.ds(0, 120), own_cols(q)], g_recv.at[it, q])
+            block = fresh.at[:, own_cols(q)]
             push(block, block, gc_send.at[it, q], gc_recv.at[it, q], other)
 
         if it + 1 < ITERS:
@@ -234,26 +227,14 @@
                 await_bytes(cur.at[it + 1, :, far_cols(q)], gc_recv.at[it, q])
             offset = offset + split_centroids(it + 1, far_half)
 
-    last = ITERS
-    outs = []
-
-    def store(cols, i):
-        copy = pltpu.make_async_copy(cur.at[last, :, cols], out_c.at[:, cols], out_sem.at[i])
-        copy.start()
-        outs.append(copy)
-
+    for n, (lo, hi) in enumerate(CHUNKS):
+        out_e[lo:hi] = energy[ITERS - 1, n, 0 : hi - lo]
     for q in range(Q):
-        store(own_cols(q), q)
-    for n, (lo, hi) in enumerate(CHUNKS):
-        out_e[lo:hi] = est[ITERS - 1, n, 2, 0 : hi - lo]
-    for q in range(Q):
-        await_bytes(cur.at[last, :, far_cols(q)], gc_recv.at[ITERS - 1, q])
-        store(far_cols(q), Q + q)
+        await_bytes(out_c.at[:, far_cols(q)], gc_recv.at[ITERS - 1, q])
 
     for it in range(ITERS):
         for n in range(2):
-            for stage in range(2):
-                await_bytes(zrecv.at[it, n, stage], z_send.at[it, n, stage])
+            await_bytes(zrecv.at[it, n, pl.ds(0, Z - 1)], z_send.at[it, n])
         await_bytes(mr0.at[it, 0], m_send.at[it, 0])
         await_bytes(mr1.at[it], m_send.at[it, 1])
         for q in range(Q):
@@ -261,8 +242,6 @@
             await_bytes(arecv.at[it, q], a_send.at[it, q])
             await_bytes(arecv.at[it, q], g_send.at[it, q])
             await_bytes(crecv.at[it, q], gc_send.at[it, q])
-    for copy in outs:
-        copy.wait()
 
 
 def local(embeddings, centroids):
@@ -277,17 +256,18 @@
             jax.ShapeDtypeStruct((pieces, PIECE), f32),
         ),
         in_specs=[pl.BlockSpec(memory_space=pl.ANY)] * 2,
-        out_specs=(pl.BlockSpec(memory_space=pl.ANY), pl.BlockSpec(memory_space=pltpu.VMEM)),
+        out_specs=(pl.BlockSpec(memory_space=pltpu.VMEM),) * 2,
         scratch_shapes=[
             vm((ROWS, D), bf16),
-            vm((ITERS + 1, K, D), f32),
+            vm((ITERS, K, D), f32),
             vm((2 * K, D), bf16),
             vm((pieces, K, PIECE), f32),
             vm((2 * K, ROWS), bf16),
             vm((K, PIECE), f32),
             vm((2, 8, PIECE), f32),
-            vm((ITERS, 2, 3, 8, PIECE), f32),
-            vm((ITERS, 2, 2, ZG - 1, 8, PIECE), f32),
+            vm((ITERS, 2, 8, PIECE), f32),
+            vm((ITERS, 2, 8, PIECE), f32),
+            vm((ITERS, 2, Z, 8, PIECE), f32),
             vm((K, D), f32),
             vm((ITERS, Q, K, CW), f32),
             vm((ITERS, Q, K, CW), f32),
@@ -296,10 +276,9 @@
             vm((ITERS, 2, 1, K), f32),
             vm((ITERS, 1, 1, K), f32),
             vm((ITERS, N * N - 1, 1, K), f32),
-            dma((3,)),
-            dma((2 * Q,)),
-            dma((ITERS, 2, 2)),
-            dma((ITERS, 2, 2)),
+            dma((9,)),
+            dma((ITERS, 2)),
+            dma((ITERS, 2)),
         ]
         + [dma((ITERS, Q))] * 8
         + [dma((ITERS, 2))] * 2,

time: 72.7 us -> 70.4 us (0.968)
  Pallas kernels: 70.6 us -> 68.2 us
    pallas_call x1, Pallas kernels: 70.6 us -> 68.2 us  [local(): pl.pallas_call(kernel, out_shape=(jax.ShapeDtypeStruct((K, D), f32), jax....]
where the time goes in v3:
time: 70.4 us; the launch traced here: 70.3 us
  Pallas kernels  68.2 us (97%)
  local copies, waits for them, and re-layouts  1.39 us (2%)
    pallas_call x1, Pallas kernels, local(): pl.pallas_call(kernel, out_shape=(jax.ShapeDtypeStruct((K, D), f32), jax....  68.2 us

profile of v3, /device:TPU:1, one launch (start us, length us, event | category | flops | bytes accessed | tf_op | source)
XLA Modules:
  0.0 70.3 jit_solution(664747257944817298)
XLA Ops:
  0.6 68.2 %shard_map.41 = (f32[128,1024]{1,0:T(8,128)S(1)}, f32[15,128]{1,0:T(8,128)S(1)}) custom-call(bf16[1920,1024]{1,0:T(8,128)(2,1)} %x_hbm.1, f32[128,1024]{1,0:T(8,128)} %c_hbm.1), custom_call_target="tpu_custom_call" | custom-call | flops 4000000000 | bytes 5000000 | tf_op jit(solution)/shard_map/pallas_call | solution.py:252
  68.9 0.8 %copy.6 = f32[128,1024]{1,0:T(8,128)} copy(f32[128,1024]{1,0:T(8,128)S(1)} %get-tuple-element.8) | data formatting | bytes 1048576
  69.7 0.6 copy.7

commit v4 on v3

--- a/solution.py
+++ b/solution.py
@@ -13,6 +13,7 @@
 ROWS = 1920
 D = 1024
 K = 128
+LANES = 128
 PIECE = 128
 HALF = D // 2
 Q = 2
@@ -34,11 +35,11 @@
 
 def kernel(
     x_hbm, c_hbm, out_c, out_e,
+    nsends, crecvs, sbufs, arecvs,
     xv, cur, cs, pbuf, ws, macc, mst, est, energy, zrecv,
-    nacc, nsend, crecv, sbuf, arecv, mbuf, mr0, mr1,
+    nacc,
     ld, z_send, z_recv,
     c_send, c_recv, a_send, a_recv, g_send, g_recv, gc_send, gc_recv,
-    m_send, m_recv,
 ):
     dp = lax.axis_index("dp")
     z = lax.axis_index("cent")
@@ -174,40 +175,32 @@
         z_join(it, 1)
         weigh(it, 1)
 
-        mass = jnp.sum(macc[...], axis=1, keepdims=True)
-        eye = lax.broadcasted_iota(jnp.int32, (K, K), 0) == lax.broadcasted_iota(jnp.int32, (K, K), 1)
-        mbuf[it, 0] = jnp.sum(jnp.where(eye, mass, 0.0), axis=0, keepdims=True)
-        push(mbuf.at[it, 0], mr0.at[it, 0], m_send.at[it, 0], m_recv.at[it, 0], other)
-
-        for q in range(Q):
-            nsend[it, q] = nacc[:, far_cols(q)] + numer(1, far_cols(q))
-            push(nsend.at[it, q], crecv.at[it, q], c_send.at[it, q], c_recv.at[it, q], other)
+        mass = jnp.broadcast_to(jnp.sum(macc[...], axis=1, keepdims=True), (K, LANES))
+
+        for q in range(Q):
+            nsends[q][it, :, 0:CW] = nacc[:, far_cols(q)] + numer(1, far_cols(q))
+            if q == 0:
+                nsends[q][it, :, CW:] = mass
+            push(nsends[q].at[it], crecvs[q].at[it], c_send.at[it, q], c_recv.at[it, q], other)
 
         for q in range(Q):
             part = nacc[:, own_cols(q)] + numer(1, own_cols(q))
-            await_bytes(crecv.at[it, q], c_recv.at[it, q])
-            sbuf[it, q] = part + crecv[it, q]
+            await_bytes(crecvs[q].at[it], c_recv.at[it, q])
+            sbufs[q][it, :, 0:CW] = part + crecvs[q][it, :, 0:CW]
+            if q == 0:
+                sbufs[q][it, :, CW:] = mass + crecvs[q][it, :, CW:]
             for d, (c, device) in enumerate(zip(chips, planes)):
                 rows = pl.ds(pl.multiple_of(c * 8, 8), 8)
-                push(sbuf.at[it, q, rows], arecv.at[it, q, d], a_send.at[it, q], a_recv.at[it, q], device)
+                push(sbufs[q].at[it, rows], arecvs[q].at[it, d], a_send.at[it, q], a_recv.at[it, q], device)
+
+        fresh = cur.at[it + 1] if it + 1 < ITERS else out_c
+        for q in range(Q):
+            await_bytes(arecvs[q].at[it], a_recv.at[it, q])
+            got = sbufs[q][it, mine] + jnp.sum(arecvs[q][it], axis=0)
             if q == 0:
-                await_bytes(mr0.at[it, 0], m_recv.at[it, 0])
-                mbuf[it, 1] = mbuf[it, 0] + mr0[it, 0]
-                for d, device in enumerate(planes):
-                    push(mbuf.at[it, 1], mr1.at[it, d], m_send.at[it, 1], m_recv.at[it, 1], device)
-
-        await_bytes(mr1.at[it], m_recv.at[it, 1])
-        total = mbuf[it, 1] + jnp.sum(mr1[it], axis=0)
-        lane = lax.broadcasted_iota(jnp.int32, (8, K), 1)
-        want = lax.broadcasted_iota(jnp.int32, (8, K), 0) + base
-        denom = jnp.sum(jnp.where(lane == want, total, 0.0), axis=1, keepdims=True) + PRIOR
-
-        fresh = cur.at[it + 1] if it + 1 < ITERS else out_c
-        for q in range(Q):
-            await_bytes(arecv.at[it, q], a_recv.at[it, q])
-            got = sbuf[it, q, mine] + jnp.sum(arecv[it, q], axis=0)
+                denom = got[:, CW : CW + 1] + PRIOR
             cols = own_cols(q)
-            fresh[mine, cols] = (got + PRIOR * cur[it, mine, cols]) / denom
+            fresh[mine, cols] = (got[:, 0:CW] + PRIOR * cur[it, mine, cols]) / denom
             block = fresh.at[mine, cols]
             for device in planes:
                 push(block, block, g_send.at[it, q], g_recv.at[it, q], device)
@@ -235,18 +228,17 @@
     for it in range(ITERS):
         for n in range(2):
             await_bytes(zrecv.at[it, n, pl.ds(0, Z - 1)], z_send.at[it, n])
-        await_bytes(mr0.at[it, 0], m_send.at[it, 0])
-        await_bytes(mr1.at[it], m_send.at[it, 1])
-        for q in range(Q):
-            await_bytes(crecv.at[it, q], c_send.at[it, q])
-            await_bytes(arecv.at[it, q], a_send.at[it, q])
-            await_bytes(arecv.at[it, q], g_send.at[it, q])
-            await_bytes(crecv.at[it, q], gc_send.at[it, q])
+        for q in range(Q):
+            await_bytes(crecvs[q].at[it], c_send.at[it, q])
+            await_bytes(arecvs[q].at[it], a_send.at[it, q])
+            await_bytes(arecvs[1].at[it], g_send.at[it, q])
+            await_bytes(crecvs[1].at[it], gc_send.at[it, q])
 
 
 def local(embeddings, centroids):
     f32, bf16 = jnp.float32, jnp.bfloat16
     pieces = ROWS // PIECE
+    widths = (CW + LANES, CW)
     vm = pltpu.VMEM
     dma = pltpu.SemaphoreType.DMA
     new, energy = pl.pallas_call(
@@ -258,6 +250,10 @@
         in_specs=[pl.BlockSpec(memory_space=pl.ANY)] * 2,
         out_specs=(pl.BlockSpec(memory_space=pltpu.VMEM),) * 2,
         scratch_shapes=[
+            [vm((ITERS, K, v), f32) for v in widths],
+            [vm((ITERS, K, v), f32) for v in widths],
+            [vm((ITERS, K, v), f32) for v in widths],
+            [vm((ITERS, N * N - 1, 8, v), f32) for v in widths],
             vm((ROWS, D), bf16),
             vm((ITERS, K, D), f32),
             vm((2 * K, D), bf16),
@@ -269,19 +265,11 @@
             vm((ITERS, 2, 8, PIECE), f32),
             vm((ITERS, 2, Z, 8, PIECE), f32),
             vm((K, D), f32),
-            vm((ITERS, Q, K, CW), f32),
-            vm((ITERS, Q, K, CW), f32),
-            vm((ITERS, Q, K, CW), f32),
-            vm((ITERS, Q, N * N - 1, 8, CW), f32),
-            vm((ITERS, 2, 1, K), f32),
-            vm((ITERS, 1, 1, K), f32),
-            vm((ITERS, N * N - 1, 1, K), f32),
             dma((9,)),
             dma((ITERS, 2)),
             dma((ITERS, 2)),
         ]
-        + [dma((ITERS, Q))] * 8
-        + [dma((ITERS, 2))] * 2,
+        + [dma((ITERS, Q))] * 8,
         compiler_params=pltpu.CompilerParams(
             collective_id=0, has_side_effects=True, vmem_limit_bytes=53 * 1024 * 1024
         ),

time: 70.4 us -> 70.6 us (level)
  no operation moved by 1% of the time
where the time goes in v4:
time: 70.6 us; the launch traced here: 70.5 us
  Pallas kernels  68.5 us (97%)
  local copies, waits for them, and re-layouts  1.39 us (2%)
    pallas_call x1, Pallas kernels, local(): pl.pallas_call(kernel, out_shape=(jax.ShapeDtypeStruct((K, D), f32), jax....  68.5 us

profile of v4, /device:TPU:1, one launch (start us, length us, event | category | flops | bytes accessed | tf_op | source)
XLA Modules:
  0.0 70.5 jit_solution(2408675860975649752)
XLA Ops:
  0.6 68.5 %shard_map.41 = (f32[128,1024]{1,0:T(8,128)S(1)}, f32[15,128]{1,0:T(8,128)S(1)}) custom-call(bf16[1920,1024]{1,0:T(8,128)(2,1)} %x_hbm.1, f32[128,1024]{1,0:T(8,128)} %c_hbm.1), custom_call_target="tpu_custom_call" | custom-call | flops 4000000000 | bytes 5000000 | tf_op jit(solution)/shard_map/pallas_call | solution.py:244
  69.1 0.8 %copy.6 = f32[128,1024]{1,0:T(8,128)} copy(f32[128,1024]{1,0:T(8,128)S(1)} %get-tuple-element.8) | data formatting | bytes 1048576
  69.9 0.6 copy.7

commit v5 on v3

--- a/solution.py
+++ b/solution.py
@@ -34,7 +34,8 @@
 
 def kernel(
     x_hbm, c_hbm, out_c, out_e,
-    xv, cur, cs, pbuf, ws, macc, mst, est, energy, zrecv,
+    msts, ests, energies, zrecvs,
+    xv, cur, cs, pbuf, ws, macc,
     nacc, nsend, crecv, sbuf, arecv, mbuf, mr0, mr1,
     ld, z_send, z_recv,
     c_send, c_recv, a_send, a_recv, g_send, g_recv, gc_send, gc_recv,
@@ -103,8 +104,8 @@
         p = jnp.exp(l - m)
         s = jnp.sum(p, axis=0, keepdims=True)
         pbuf[r] = p
-        mst[n, i : i + 1] = m
-        est[it, n, i : i + 1] = m + jnp.log(s)
+        msts[n][i : i + 1] = m
+        ests[n][it, i : i + 1] = m + jnp.log(s)
 
     def product(rows, cols):
         both = dot(cs[:, cols], xv[rows, cols], NT)
@@ -124,18 +125,18 @@
 
     def z_push(it, n):
         for device in along_z:
-            push(est.at[it, n], zrecv.at[it, n, z], z_send.at[it, n], z_recv.at[it, n], device)
-        zrecv[it, n, z] = est[it, n]
+            push(ests[n].at[it], zrecvs[n].at[it, z], z_send.at[it, n], z_recv.at[it, n], device)
+        zrecvs[n][it, z] = ests[n][it]
 
     def z_join(it, n):
-        await_bytes(zrecv.at[it, n, pl.ds(0, Z - 1)], z_recv.at[it, n])
-        e = zrecv[it, n]
+        await_bytes(zrecvs[n].at[it, pl.ds(0, Z - 1)], z_recv.at[it, n])
+        e = zrecvs[n][it]
         m = jnp.max(e, axis=0)
-        energy[it, n] = m + jnp.log(jnp.sum(jnp.exp(e - m[None]), axis=0))
+        energies[n][it] = m + jnp.log(jnp.sum(jnp.exp(e - m[None]), axis=0))
 
     def weigh(it, n):
         lo, hi = CHUNKS[n]
-        f = jnp.exp(mst[n] - energy[it, n])
+        f = jnp.exp(msts[n][...] - energies[n][it])
         for r in range(lo, hi):
             w = pbuf[r] * f[r - lo : r - lo + 1]
             hi_w, lo_w = split(w)
@@ -149,12 +150,6 @@
         rows = pl.ds(lo * PIECE, (hi - lo) * PIECE)
         both = dot(ws[:, rows], xv[rows, cols], NN)
         return both[0:K] + both[K : 2 * K]
-
-    for n, (lo, hi) in enumerate(CHUNKS):
-        if hi - lo < 8:
-            mst[n, hi - lo : 8] = jnp.zeros((8 - hi + lo, PIECE), jnp.float32)
-            for it in range(ITERS):
-                est[it, n, hi - lo : 8] = jnp.zeros((8 - hi + lo, PIECE), jnp.float32)
 
     load_c.wait()
     offset = split_centroids(0, pl.ds(0, D))
@@ -185,16 +180,16 @@
 
         for q in range(Q):
             part = nacc[:, own_cols(q)] + numer(1, own_cols(q))
+            if q == 0:
+                await_bytes(mr0.at[it, 0], m_recv.at[it, 0])
+                mbuf[it, 1] = mbuf[it, 0] + mr0[it, 0]
+                for d, device in enumerate(planes):
+                    push(mbuf.at[it, 1], mr1.at[it, d], m_send.at[it, 1], m_recv.at[it, 1], device)
             await_bytes(crecv.at[it, q], c_recv.at[it, q])
             sbuf[it, q] = part + crecv[it, q]
             for d, (c, device) in enumerate(zip(chips, planes)):
                 rows = pl.ds(pl.multiple_of(c * 8, 8), 8)
                 push(sbuf.at[it, q, rows], arecv.at[it, q, d], a_send.at[it, q], a_recv.at[it, q], device)
-            if q == 0:
-                await_bytes(mr0.at[it, 0], m_recv.at[it, 0])
-                mbuf[it, 1] = mbuf[it, 0] + mr0[it, 0]
-                for d, device in enumerate(planes):
-                    push(mbuf.at[it, 1], mr1.at[it, d], m_send.at[it, 1], m_recv.at[it, 1], device)
 
         await_bytes(mr1.at[it], m_recv.at[it, 1])
         total = mbuf[it, 1] + jnp.sum(mr1[it], axis=0)
@@ -228,13 +223,13 @@
             offset = offset + split_centroids(it + 1, far_half)
 
     for n, (lo, hi) in enumerate(CHUNKS):
-        out_e[lo:hi] = energy[ITERS - 1, n, 0 : hi - lo]
+        out_e[lo:hi] = energies[n][ITERS - 1]
     for q in range(Q):
         await_bytes(out_c.at[:, far_cols(q)], gc_recv.at[ITERS - 1, q])
 
     for it in range(ITERS):
         for n in range(2):
-            await_bytes(zrecv.at[it, n, pl.ds(0, Z - 1)], z_send.at[it, n])
+            await_bytes(zrecvs[n].at[it, pl.ds(0, Z - 1)], z_send.at[it, n])
         await_bytes(mr0.at[it, 0], m_send.at[it, 0])
         await_bytes(mr1.at[it], m_send.at[it, 1])
         for q in range(Q):
@@ -247,6 +242,7 @@
 def local(embeddings, centroids):
     f32, bf16 = jnp.float32, jnp.bfloat16
     pieces = ROWS // PIECE
+    sizes = [hi - lo for lo, hi in CHUNKS]
     vm = pltpu.VMEM
     dma = pltpu.SemaphoreType.DMA
     new, energy = pl.pallas_call(
@@ -258,16 +254,16 @@
         in_specs=[pl.BlockSpec(memory_space=pl.ANY)] * 2,
         out_specs=(pl.BlockSpec(memory_space=pltpu.VMEM),) * 2,
         scratch_shapes=[
+            [vm((v, PIECE), f32) for v in sizes],
+            [vm((ITERS, v, PIECE), f32) for v in sizes],
+            [vm((ITERS, v, PIECE), f32) for v in sizes],
+            [vm((ITERS, Z, v, PIECE), f32) for v in sizes],
             vm((ROWS, D), bf16),
             vm((ITERS, K, D), f32),
             vm((2 * K, D), bf16),
             vm((pieces, K, PIECE), f32),
             vm((2 * K, ROWS), bf16),
             vm((K, PIECE), f32),
-            vm((2, 8, PIECE), f32),
-            vm((ITERS, 2, 8, PIECE), f32),
-            vm((ITERS, 2, 8, PIECE), f32),
-            vm((ITERS, 2, Z, 8, PIECE), f32),
             vm((K, D), f32),
             vm((ITERS, Q, K, CW), f32),
             vm((ITERS, Q, K, CW), f32),

time: 70.4 us -> 69.8 us (level)
  no operation moved by 1% of the time
where the time goes in v5:
time: 69.8 us; the launch traced here: 69.7 us
  Pallas kernels  67.6 us (97%)
  local copies, waits for them, and re-layouts  1.39 us (2%)
    pallas_call x1, Pallas kernels, local(): pl.pallas_call(kernel, out_shape=(jax.ShapeDtypeStruct((K, D), f32), jax....  67.6 us

profile of v5, /device:TPU:1, one launch (start us, length us, event | category | flops | bytes accessed | tf_op | source)
XLA Modules:
  0.0 69.7 jit_solution(7454673307339683846)
XLA Ops:
  0.6 67.6 %shard_map.41 = (f32[128,1024]{1,0:T(8,128)S(1)}, f32[15,128]{1,0:T(8,128)S(1)}) custom-call(bf16[1920,1024]{1,0:T(8,128)(2,1)} %x_hbm.1, f32[128,1024]{1,0:T(8,128)} %c_hbm.1), custom_call_target="tpu_custom_call" | custom-call | flops 4000000000 | bytes 5000000 | tf_op jit(solution)/shard_map/pallas_call | solution.py:248
  68.3 0.8 %copy.6 = f32[128,1024]{1,0:T(8,128)} copy(f32[128,1024]{1,0:T(8,128)S(1)} %get-tuple-element.8) | data formatting | bytes 1048576
  69.1 0.6 copy.7

commit v6 on v5

--- a/solution.py
+++ b/solution.py
@@ -52,11 +52,11 @@
     def chip_at(dx, dy):
         return lax.rem(cy + dy, N) * N + lax.rem(cx + dx, N)
 
-    moves = [(dx, dy) for dx in range(N) for dy in range(N) if dx or dy]
-    moves.sort(key=lambda v: -(min(v[0], N - v[0]) + min(v[1], N - v[1])))
-    chips = [chip_at(dx, dy) for dx, dy in moves]
-    planes = [(2 * c + core, z) for c in chips]
-    along_z = [(dp, lax.rem(z + d, Z)) for d in sorted(range(1, Z), key=lambda d: -min(d, Z - d))]
+    def plane_chip(d):
+        return chip_at(lax.rem(d, N), d // N)
+
+    def along_z(d):
+        return (dp, lax.rem(z + d, Z))
 
     def push(src, dst, send, recv, device):
         pltpu.make_async_remote_copy(
@@ -76,9 +76,16 @@
         loads[-1].start()
 
     barrier = pltpu.get_barrier_semaphore()
-    peers = [other] + planes + along_z
-    for device in peers:
+
+    def greet(device):
         pl.semaphore_signal(barrier, inc=1, device_id=device, device_id_type=MESH)
+
+    greet(other)
+
+    @pl.loop(1, N * N)
+    def _(d):
+        greet((2 * plane_chip(d) + core, z))
+        greet(along_z(d))
 
     def own_cols(q):
         return pl.ds(pl.multiple_of(core * HALF + q * CW, CW), CW)
@@ -124,8 +131,10 @@
                 stats(it, n, part if it == 0 else part + pbuf[r0 + j], r0 + j)
 
     def z_push(it, n):
-        for device in along_z:
-            push(ests[n].at[it], zrecvs[n].at[it, z], z_send.at[it, n], z_recv.at[it, n], device)
+        @pl.loop(1, Z)
+        def _(d):
+            push(ests[n].at[it], zrecvs[n].at[it, z], z_send.at[it, n], z_recv.at[it, n], along_z(d))
+
         zrecvs[n][it, z] = ests[n][it]
 
     def z_join(it, n):
@@ -157,7 +166,7 @@
         for n in range(2):
             logits(it, n)
             if it == 0 and n == 0:
-                pl.semaphore_wait(barrier, len(peers))
+                pl.semaphore_wait(barrier, N * N - 1 + Z)
             z_push(it, n)
         macc[...] = jnp.zeros_like(macc)
         z_join(it, 0)
@@ -183,13 +192,21 @@
             if q == 0:
                 await_bytes(mr0.at[it, 0], m_recv.at[it, 0])
                 mbuf[it, 1] = mbuf[it, 0] + mr0[it, 0]
-                for d, device in enumerate(planes):
-                    push(mbuf.at[it, 1], mr1.at[it, d], m_send.at[it, 1], m_recv.at[it, 1], device)
+
+                @pl.loop(1, N * N)
+                def _(d):
+                    device = (2 * plane_chip(d) + core, z)
+                    push(mbuf.at[it, 1], mr1.at[it, d - 1], m_send.at[it, 1], m_recv.at[it, 1], device)
+
             await_bytes(crecv.at[it, q], c_recv.at[it, q])
             sbuf[it, q] = part + crecv[it, q]
-            for d, (c, device) in enumerate(zip(chips, planes)):
+
+            @pl.loop(1, N * N)
+            def _(d):
+                c = plane_chip(d)
                 rows = pl.ds(pl.multiple_of(c * 8, 8), 8)
-                push(sbuf.at[it, q, rows], arecv.at[it, q, d], a_send.at[it, q], a_recv.at[it, q], device)
+                push(sbuf.at[it, q, rows], arecv.at[it, q, d - 1], a_send.at[it, q], a_recv.at[it, q], (2 * c + core, z))
+
 
         await_bytes(mr1.at[it], m_recv.at[it, 1])
         total = mbuf[it, 1] + jnp.sum(mr1[it], axis=0)
@@ -204,8 +221,11 @@
             cols = own_cols(q)
             fresh[mine, cols] = (got + PRIOR * cur[it, mine, cols]) / denom
             block = fresh.at[mine, cols]
-            for device in planes:
-                push(block, block, g_send.at[it, q], g_recv.at[it, q], device)
+
+            @pl.loop(1, N * N)
+            def _(d):
+                push(block, block, g_send.at[it, q], g_recv.at[it, q], (2 * plane_chip(d) + core, z))
+
         for q in range(Q):
             await_bytes(fresh.at[pl.ds(0, 120), own_cols(q)], g_recv.at[it, q])
             block = fresh.at[:, own_cols(q)]

time: 69.8 us -> 73.8 us (1.057)
  Pallas kernels: 67.6 us -> 71.6 us
    pallas_call x1, Pallas kernels: 67.6 us -> 71.6 us  [local(): pl.pallas_call(kernel, out_shape=(jax.ShapeDtypeStruct((K, D), f32), jax....]
where the time goes in v6:
time: 73.8 us; the launch traced here: 73.7 us
  Pallas kernels  71.6 us (97%)
  local copies, waits for them, and re-layouts  1.39 us (2%)
    pallas_call x1, Pallas kernels, local(): pl.pallas_call(kernel, out_shape=(jax.ShapeDtypeStruct((K, D), f32), jax....  71.6 us

profile of v6, /device:TPU:1, one launch (start us, length us, event | category | flops | bytes accessed | tf_op | source)
XLA Modules:
  0.0 73.7 jit_solution(10804620133001639782)
XLA Ops:
  0.6 71.6 %shard_map.41 = (f32[128,1024]{1,0:T(8,128)S(1)}, f32[15,128]{1,0:T(8,128)S(1)}) custom-call(bf16[1920,1024]{1,0:T(8,128)(2,1)} %x_hbm.1, f32[128,1024]{1,0:T(8,128)} %c_hbm.1), custom_call_target="tpu_custom_call" | custom-call | flops 4000000000 | bytes 5000000 | tf_op jit(solution)/shard_map/pallas_call | solution.py:268
  72.3 0.8 %copy.6 = f32[128,1024]{1,0:T(8,128)} copy(f32[128,1024]{1,0:T(8,128)S(1)} %get-tuple-element.8) | data formatting | bytes 1048576
  73.1 0.6 copy.7

commit v7 on v5

--- a/solution.py
+++ b/solution.py
@@ -86,8 +86,6 @@
     def far_cols(q):
         return pl.ds(pl.multiple_of((1 - core) * HALF + q * CW, CW), CW)
 
-    own_half = pl.ds(pl.multiple_of(core * HALF, HALF), HALF)
-    far_half = pl.ds(pl.multiple_of((1 - core) * HALF, HALF), HALF)
     base = pl.multiple_of(chip * 8, 8)
     mine = pl.ds(base, 8)
 
@@ -118,7 +116,7 @@
             rows = pl.ds(r0 * PIECE, size * PIECE)
             if it == 0:
                 loads[r0 // 2].wait()
-            l = product(rows, pl.ds(0, D) if it == 0 else far_half) - offset
+            l = product(rows, pl.ds(0, D) if it == 0 else far_cols(1)) - offset
             for j in range(size):
                 part = l[:, j * PIECE : (j + 1) * PIECE]
                 stats(it, n, part if it == 0 else part + pbuf[r0 + j], r0 + j)
@@ -206,26 +204,32 @@
             block = fresh.at[mine, cols]
             for device in planes:
                 push(block, block, g_send.at[it, q], g_recv.at[it, q], device)
+        def partial(parts, add):
+            for r0 in range(0, ROWS // PIECE, 2):
+                size = min(2, ROWS // PIECE - r0)
+                l = sum(product(pl.ds(r0 * PIECE, size * PIECE), cols) for cols in parts)
+                for j in range(size):
+                    new = l[:, j * PIECE : (j + 1) * PIECE]
+                    pbuf[r0 + j] = pbuf[r0 + j] + new if add else new
+
+        more = it + 1 < ITERS
         for q in range(Q):
             await_bytes(fresh.at[pl.ds(0, 120), own_cols(q)], g_recv.at[it, q])
             block = fresh.at[:, own_cols(q)]
             push(block, block, gc_send.at[it, q], gc_recv.at[it, q], other)
-
-        if it + 1 < ITERS:
-            offset = split_centroids(it + 1, own_half)
-            for r0 in range(0, ROWS // PIECE, 2):
-                size = min(2, ROWS // PIECE - r0)
-                l = product(pl.ds(r0 * PIECE, size * PIECE), own_half)
-                for j in range(size):
-                    pbuf[r0 + j] = l[:, j * PIECE : (j + 1) * PIECE]
-            for q in range(Q):
-                await_bytes(cur.at[it + 1, :, far_cols(q)], gc_recv.at[it, q])
-            offset = offset + split_centroids(it + 1, far_half)
+            if more and q == 0:
+                offset = split_centroids(it + 1, own_cols(0))
+                partial([own_cols(0)], False)
+        await_bytes(fresh.at[:, far_cols(0)], gc_recv.at[it, 0])
+        if more:
+            offset = offset + split_centroids(it + 1, own_cols(1)) + split_centroids(it + 1, far_cols(0))
+            partial([own_cols(1), far_cols(0)], True)
+        await_bytes(fresh.at[:, far_cols(1)], gc_recv.at[it, 1])
+        if more:
+            offset = offset + split_centroids(it + 1, far_cols(1))
 
     for n, (lo, hi) in enumerate(CHUNKS):
         out_e[lo:hi] = energies[n][ITERS - 1]
-    for q in range(Q):
-        await_bytes(out_c.at[:, far_cols(q)], gc_recv.at[ITERS - 1, q])
 
     for it in range(ITERS):
         for n in range(2):

time: 69.8 us -> 69.7 us (level)
  no operation moved by 1% of the time
where the time goes in v7:
time: 69.7 us; the launch traced here: 69.6 us
  Pallas kernels  67.6 us (97%)
  local copies, waits for them, and re-layouts  1.39 us (2%)
    pallas_call x1, Pallas kernels, local(): pl.pallas_call(kernel, out_shape=(jax.ShapeDtypeStruct((K, D), f32), jax....  67.6 us
    unnamed x2, local copies, waits for them, and re-layouts  1.39 us

profile of v7, /device:TPU:1, one launch (start us, length us, event | category | flops | bytes accessed | tf_op | source)
XLA Modules:
  0.0 69.6 jit_solution(13226547001896539688)
XLA Ops:
  0.6 67.6 %shard_map.41 = (f32[128,1024]{1,0:T(8,128)S(1)}, f32[15,128]{1,0:T(8,128)S(1)}) custom-call(bf16[1920,1024]{1,0:T(8,128)(2,1)} %x_hbm.1, f32[128,1024]{1,0:T(8,128)} %c_hbm.1), custom_call_target="tpu_custom_call" | custom-call | flops 4000000000 | bytes 5000000 | tf_op jit(solution)/shard_map/pallas_call | solution.py:252
  68.2 0.8 %copy.6 = f32[128,1024]{1,0:T(8,128)} copy(f32[128,1024]{1,0:T(8,128)S(1)} %get-tuple-element.8) | data formatting | bytes 1048576
  69.0 0.6 copy.7

commit v8 on v7

--- a/solution.py
+++ b/solution.py
@@ -54,9 +54,9 @@
 
     moves = [(dx, dy) for dx in range(N) for dy in range(N) if dx or dy]
     moves.sort(key=lambda v: -(min(v[0], N - v[0]) + min(v[1], N - v[1])))
-    chips = [chip_at(dx, dy) for dx, dy in moves]
+    chips = [chip_at(dx + core * (2 * N - 2 * dx), dy + core * (2 * N - 2 * dy)) for dx, dy in moves]
     planes = [(2 * c + core, z) for c in chips]
-    along_z = [(dp, lax.rem(z + d, Z)) for d in sorted(range(1, Z), key=lambda d: -min(d, Z - d))]
+    along_z = [(dp, lax.rem(z + d + core * (2 * Z - 2 * d), Z)) for d in sorted(range(1, Z), key=lambda d: -min(d, Z - d))]
 
     def push(src, dst, send, recv, device):
         pltpu.make_async_remote_copy(

time: 69.7 us -> 69.7 us (level)
  no operation moved by 1% of the time
where the time goes in v8:
time: 69.7 us; the launch traced here: 69.6 us
  Pallas kernels  67.6 us (97%)
  local copies, waits for them, and re-layouts  1.39 us (2%)
    pallas_call x1, Pallas kernels, local(): pl.pallas_call(kernel, out_shape=(jax.ShapeDtypeStruct((K, D), f32), jax....  67.6 us
    unnamed x2, local copies, waits for them, and re-layouts  1.39 us

profile of v8, /device:TPU:1, one launch (start us, length us, event | category | flops | bytes accessed | tf_op | source)
XLA Modules:
  0.0 69.6 jit_solution(11561821558098223323)
XLA Ops:
  0.6 67.6 %shard_map.41 = (f32[128,1024]{1,0:T(8,128)S(1)}, f32[15,128]{1,0:T(8,128)S(1)}) custom-call(bf16[1920,1024]{1,0:T(8,128)(2,1)} %x_hbm.1, f32[128,1024]{1,0:T(8,128)} %c_hbm.1), custom_call_target="tpu_custom_call" | custom-call | flops 4000000000 | bytes 5000000 | tf_op jit(solution)/shard_map/pallas_call | solution.py:252
  68.2 0.8 %copy.6 = f32[128,1024]{1,0:T(8,128)} copy(f32[128,1024]{1,0:T(8,128)S(1)} %get-tuple-element.8) | data formatting | bytes 1048576
  69.0 0.6 copy.7

commit v9 on v7

--- a/solution.py
+++ b/solution.py
@@ -17,7 +17,7 @@
 HALF = D // 2
 Q = 2
 CW = HALF // Q
-CHUNKS = ((0, 8), (8, 15))
+CHUNKS = ((0, 10), (10, 15))
 NT = (((1,), (1,)), ((), ()))
 NN = (((1,), (0,)), ((), ()))
 

time: 69.7 us -> 69.9 us (level)
  no operation moved by 1% of the time
where the time goes in v9:
time: 69.9 us; the launch traced here: 69.8 us
  Pallas kernels  67.7 us (97%)
  local copies, waits for them, and re-layouts  1.39 us (2%)
    pallas_call x1, Pallas kernels, local(): pl.pallas_call(kernel, out_shape=(jax.ShapeDtypeStruct((K, D), f32), jax....  67.7 us

profile of v9, /device:TPU:1, one launch (start us, length us, event | category | flops | bytes accessed | tf_op | source)
XLA Modules:
  0.0 69.8 jit_solution(4855402505102940168)
XLA Ops:
  0.6 67.7 %shard_map.41 = (f32[128,1024]{1,0:T(8,128)S(1)}, f32[15,128]{1,0:T(8,128)S(1)}) custom-call(bf16[1920,1024]{1,0:T(8,128)(2,1)} %x_hbm.1, f32[128,1024]{1,0:T(8,128)} %c_hbm.1), custom_call_target="tpu_custom_call" | custom-call | flops 4000000000 | bytes 5000000 | tf_op jit(solution)/shard_map/pallas_call | solution.py:252
  68.4 0.8 %copy.6 = f32[128,1024]{1,0:T(8,128)} copy(f32[128,1024]{1,0:T(8,128)S(1)} %get-tuple-element.8) | data formatting | bytes 1048576
  69.2 0.6 copy.7
